TPU v7x, 32 devices: a whole 2x2x4 slice. The times are simulated.
32 devices in a mesh: img: 4 (over y, core), rows: 2 (over x), scale: 4 (over z).
Axes of the slice: x: 2, y: 2, z: 4, core: 2. Of those that a mesh axis runs over, the one named last changes fastest.
Arguments:
- block_input: bfloat16 [4, 16, 64, 768], P('img', ('rows', 'scale')), may hold values from -6 to 6
- pre_gain: bfloat16 [768], replicated, may hold values from 0.5 to 1.5
- pre_shift: bfloat16 [768], replicated, may hold values from -0.625 to 0.625
- qkv_weight: bfloat16 [768, 2304], replicated, may hold values from -0.21875 to 0.21875
- qv_bias: bfloat16 [1536], replicated, may hold values from -0.125 to 0.125
- rel_rows: bfloat16 [31, 64], replicated, may hold values from -0.875 to 0.875
- rel_cols: bfloat16 [127, 64], replicated, may hold values from -0.875 to 0.875
- proj_weight: bfloat16 [768, 768], replicated, may hold values from -2.5 to 2.5
- proj_bias: bfloat16 [768], replicated, may hold values from -0.625 to 0.625
- mid_gain: bfloat16 [768], replicated, may hold values from 0.5 to 1.5
- mid_shift: bfloat16 [768], replicated, may hold values from -0.625 to 0.625
- fc1_weight: bfloat16 [768, 3072], replicated, may hold values from -0.21875 to 0.21875
- fc1_bias: bfloat16 [3072], replicated, may hold values from -0.625 to 0.625
- fc2_weight: bfloat16 [3072, 768], replicated, may hold values from -0.109375 to 0.109375
- fc2_bias: bfloat16 [768], replicated, may hold values from -0.625 to 0.625
- deconv_first: bfloat16 [768, 1536], replicated, may hold values from -0.21875 to 0.21875
- first_bias: bfloat16 [384], replicated, may hold values from -0.625 to 0.625
- upnorm_gain: bfloat16 [384], replicated, may hold values from 0.5 to 1.5
- upnorm_shift: bfloat16 [384], replicated, may hold values from -0.625 to 0.625
- deconv_second: bfloat16 [768, 384], replicated, may hold values from -0.3125 to 0.3125
- second_bias: bfloat16 [192], replicated, may hold values from -0.625 to 0.625
- deconv_eight: bfloat16 [768, 1536], replicated, may hold values from -0.21875 to 0.21875
- eight_bias: bfloat16 [384], replicated, may hold values from -0.625 to 0.625
- lateral_four: bfloat16 [256, 192], replicated, may hold values from -0.4375 to 0.4375
- lateral_eight: bfloat16 [256, 384], replicated, may hold values from -0.3125 to 0.3125
- lateral_sixteen: bfloat16 [256, 768], replicated, may hold values from -0.21875 to 0.21875
- lateral_thirty: bfloat16 [256, 768], replicated, may hold values from -0.21875 to 0.21875
- lateral_gain: bfloat16 [4, 256], replicated, may hold values from 0.5 to 1.5
- lateral_shift: bfloat16 [4, 256], replicated, may hold values from -0.625 to 0.625
- smooth_weight: bfloat16 [4, 2304, 256], replicated, may hold values from -0.125 to 0.125
- output_gain: bfloat16 [4, 256], replicated, may hold values from 0.5 to 1.5
- grad_four: bfloat16 [4, 64, 256, 256], P('img', 'rows'), may hold values from -6 to 6
- grad_eight: bfloat16 [4, 32, 128, 256], P('img', 'rows'), may hold values from -6 to 6
- grad_sixteen: bfloat16 [4, 16, 64, 256], P('img', 'rows'), may hold values from -6 to 6
- grad_thirty: bfloat16 [4, 8, 32, 256], P('img', 'rows'), may hold values from -6 to 6
- anchor_four: int32 [4, 64, 256], P('img', 'rows'), may hold values 0 or 1
- anchor_eight: int32 [4, 32, 128], P('img', 'rows'), may hold values 0 or 1
- anchor_sixteen: int32 [4, 16, 64], P('img', 'rows'), may hold values 0 or 1
- anchor_thirty: int32 [4, 8, 32], P('img', 'rows'), may hold values 0 or 1
- roi_mask: int32 [4, 16, 64], P('img', 'rows'), may hold values 0 or 1
Outputs:
- block_output: bfloat16 [4, 16, 64, 768], P('img', ('rows', 'scale'))
- input_grad: float32 [4, 16, 64, 768], P('img', ('rows', 'scale'))
- pre_gain_grad: float32 [768], replicated
- pre_shift_grad: float32 [768], replicated
- qkv_weight_grad: float32 [1769472], P(('img', 'rows', 'scale'))
- qv_bias_grad: float32 [1536], replicated
- rel_rows_grad: float32 [31, 64], replicated
- rel_cols_grad: float32 [127, 64], replicated
- proj_weight_grad: float32 [589824], P(('img', 'rows', 'scale'))
- proj_bias_grad: float32 [768], replicated
- mid_gain_grad: float32 [768], replicated
- mid_shift_grad: float32 [768], replicated
- fc1_weight_grad: float32 [2359296], P(('img', 'rows', 'scale'))
- fc1_bias_grad: float32 [3072], replicated
- fc2_weight_grad: float32 [2359296], P(('img', 'rows', 'scale'))
- fc2_bias_grad: float32 [768], replicated
- deconv_first_grad: float32 [1179648], P(('img', 'rows', 'scale'))
- first_bias_grad: float32 [384], replicated
- upnorm_gain_grad: float32 [384], replicated
- upnorm_shift_grad: float32 [384], replicated
- deconv_second_grad: float32 [294912], P(('img', 'rows', 'scale'))
- second_bias_grad: float32 [192], replicated
- deconv_eight_grad: float32 [1179648], P(('img', 'rows', 'scale'))
- eight_bias_grad: float32 [384], replicated
- lateral_four_grad: float32 [49152], P(('img', 'rows', 'scale'))
- lateral_eight_grad: float32 [98304], P(('img', 'rows', 'scale'))
- lateral_sixteen_grad: float32 [196608], P(('img', 'rows', 'scale'))
- lateral_thirty_grad: float32 [196608], P(('img', 'rows', 'scale'))
- lateral_gain_grad: float32 [4, 256], replicated
- lateral_shift_grad: float32 [4, 256], replicated
- smooth_weight_grad: float32 [2359296], P(('img', 'rows', 'scale'))
- output_gain_grad: float32 [4, 256], replicated
All inputs are finite; a program needn't handle non-finite values. No bound on the sum of `anchor_four` or of `anchor_eight` or of `anchor_sixteen` or of `anchor_thirty` or of `roi_mask` on one device may be relied on, other than what follows from the above.
Results may differ from a plain program's by a relative error of at most 0.024.
Values may be sent and summed in bfloat16 or wider, within the bound.
A program may use at most 320 MiB of HBM per device.

v0:
```python
from functools import partial

import jax
import jax.numpy as jnp
from jax import lax
from jax.sharding import PartitionSpec as P

highest = lax.Precision.HIGHEST
norm_eps = 1e-06
wide_type = jnp.float32
narrow_type = jnp.bfloat16


def padded_2(value, sides, width):
    for axis, dim in sides:
        size, length = (lax.axis_size(axis), value.shape[dim])
        up = [(i, (i + 1) % size) for i in range(size - 1)]
        down = [(j, i) for i, j in up]
        last = lax.slice_in_dim(value, length - width, length, axis=dim)
        initial = lax.slice_in_dim(value, 0, width, axis=dim)
        before = lax.ppermute(last, axis, up)
        after = lax.ppermute(initial, axis, down)
        value = jnp.concatenate([before, value, after], axis=dim)
    return value


def as_sent(value):
    return jax.tree.map(lambda a: a.astype(jnp.bfloat16) if a.dtype == jnp.float32 else a, value)


def layer_norm(values, gain_vec, shift_vec):
    centre = values - jnp.mean(values, axis=-1, keepdims=True)
    spread = jnp.mean(centre * centre, axis=-1, keepdims=True)
    return centre * lax.rsqrt(spread + norm_eps) * gain_vec + shift_vec


def scaled_norm(values, gain_vec):
    centre = values - jnp.mean(values, axis=-1, keepdims=True)
    spread = jnp.mean(centre * centre, axis=-1, keepdims=True)
    return centre * lax.rsqrt(spread + norm_eps) * gain_vec


def apply_right(values, weight):
    return jnp.einsum("...c,cn->...n", values, weight, preferred_element_type=wide_type)


def apply_left(values, weight):
    return jnp.einsum("...c,nc->...n", values, weight, preferred_element_type=wide_type)


def outer_sum(left_side, right_side):
    return jnp.einsum("...a,...b->ab", left_side, right_side, preferred_element_type=wide_type)


def position_sum(values):
    return jnp.sum(values, axis=(0, 1, 2), dtype=wide_type)


def unfold_taps(values):
    images, row_count, col_count, tap_count = values.shape
    channels = tap_count // 4
    values = values.reshape(images, row_count, col_count, 2, 2, channels).transpose(
        0, 1, 3, 2, 4, 5
    )
    return values.reshape(images, 2 * row_count, 2 * col_count, channels)


def fold_taps(values):
    images, row_count, col_count, channels = values.shape
    values = values.reshape(images, row_count // 2, 2, col_count // 2, 2, channels).transpose(
        0, 1, 3, 2, 4, 5
    )
    return values.reshape(images, row_count // 2, col_count // 2, 4 * channels)


def offset_hot(q_start, q_count, k_count, length):
    offsets = (
        (q_start + jnp.arange(q_count, dtype=jnp.int32))[:, None]
        - jnp.arange(k_count, dtype=jnp.int32)[None, :]
        + length
        - 1
    )
    return (
        offsets[:, :, None] == jnp.arange(2 * length - 1, dtype=jnp.int32)[None, None, :]
    ).astype(wide_type)


def offset_rows(onehot, table_in):
    return jnp.einsum("ijr,rc->ijc", onehot, table_in, precision=highest)


def per_head(values, head_count, head_size):
    return values.reshape(values.shape[:-1] + (head_count, head_size))


def attention_scores(query_img, key_img, row_table, col_table):
    q_rows, col_count, head_count, head_size = query_img.shape
    k_rows = key_img.shape[0]
    plain_part = jnp.einsum(
        "xyhc,abhc->hxyab", query_img, key_img, preferred_element_type=wide_type
    ) * head_size ** (-0.5)
    query_wide = query_img.astype(wide_type)
    by_row = jnp.einsum("xyhc,xac->hxya", query_wide, row_table, precision=highest)
    by_col = jnp.einsum("xyhc,ybc->hxyb", query_wide, col_table, precision=highest)
    summed = plain_part + by_row[:, :, :, :, None] + by_col[:, :, :, None, :]
    return summed.reshape(head_count, q_rows * col_count, k_rows * col_count)


def score_back(score_grad, query_img, key_flat, row_table, col_table):
    q_rows, col_count, head_count, head_size = query_img.shape
    k_rows = row_table.shape[1]
    blocks = score_grad.reshape(head_count, q_rows, col_count, k_rows, col_count)
    by_row = jnp.sum(blocks, axis=4, dtype=wide_type)
    by_col = jnp.sum(blocks, axis=3, dtype=wide_type)
    plain_part = jnp.einsum(
        "hqk,khc->qhc", score_grad, key_flat, preferred_element_type=wide_type
    ) * head_size ** (-0.5)
    plain_part = plain_part.reshape(query_img.shape)
    query_wide = query_img.astype(wide_type)
    rel_part = jnp.einsum("hxya,xac->xyhc", by_row, row_table, precision=highest) + jnp.einsum(
        "hxyb,ybc->xyhc", by_col, col_table, precision=highest
    )
    row_part = jnp.einsum("hxya,xyhc->xac", by_row, query_wide, precision=highest)
    col_part = jnp.einsum("hxyb,xyhc->ybc", by_col, query_wide, precision=highest)
    return (plain_part + rel_part, row_part, col_part)


def smooth_forward(values, weight, extend):
    row_count, col_count, channels = (values.shape[1], values.shape[2], values.shape[3])
    padded = jnp.pad(extend(values), ((0, 0), (0, 0), (1, 1), (0, 0)))
    summed = jnp.zeros(values.shape[:3] + (weight.shape[1],), wide_type)
    for offset_tap in range(9):
        row_step, col_step = (offset_tap // 3, offset_tap % 3)
        window = padded[:, row_step : row_step + row_count, col_step : col_step + col_count]
        summed = summed + apply_right(
            window, weight[offset_tap * channels : (offset_tap + 1) * channels]
        )
    return (summed, padded)


def smooth_backward(padded, upstream, weight, extend):
    row_count, col_count = (upstream.shape[1], upstream.shape[2])
    channels = padded.shape[3]
    beside_all = jnp.pad(extend(upstream), ((0, 0), (0, 0), (1, 1), (0, 0)))
    input_grad = jnp.zeros(upstream.shape[:3] + (channels,), wide_type)
    pieces = []
    for offset_tap in range(9):
        row_step, col_step = (offset_tap // 3, offset_tap % 3)
        window = padded[:, row_step : row_step + row_count, col_step : col_step + col_count]
        pieces.append(outer_sum(window, upstream))
        back_window = beside_all[
            :, 2 - row_step : 2 - row_step + row_count, 2 - col_step : 2 - col_step + col_count
        ]
        input_grad = input_grad + apply_left(
            back_window, weight[offset_tap * channels : (offset_tap + 1) * channels]
        )
    return (input_grad, jnp.concatenate(pieces, axis=0))


def finish_level(source, lateral, gain_vec, shift_vec, smooth, out_gain, loss_weight, extend):
    reduced = apply_left(source, lateral)
    normed, norm_pull = jax.vjp(
        layer_norm, reduced, gain_vec.astype(wide_type), shift_vec.astype(wide_type)
    )
    normed_low = normed.astype(narrow_type)
    smoothed, padded = smooth_forward(normed_low, smooth, extend)
    level_out, out_pull = jax.vjp(scaled_norm, smoothed, out_gain.astype(wide_type))
    smoothed_grad, out_gain_grad = out_pull(loss_weight)
    smoothed_low = smoothed_grad.astype(narrow_type)
    normed_grad, smooth_grad = smooth_backward(padded, smoothed_low, smooth, extend)
    reduced_grad, gain_grad, shift_grad = norm_pull(normed_grad)
    reduced_low = reduced_grad.astype(narrow_type)
    lateral_grad = outer_sum(reduced_low, source)
    source_grad = apply_right(reduced_low, lateral)
    return (source_grad, lateral_grad, gain_grad, shift_grad, smooth_grad, out_gain_grad)


def squash(pre_values, gain_vec, shift_vec):
    return jax.nn.gelu(layer_norm(pre_values, gain_vec, shift_vec), approximate=False)


def pyramid_level(scale_level, extend, strip, loss_weight, pyramid):
    (
        deconv_first,
        first_bias,
        upnorm_gain,
        upnorm_shift,
        deconv_second,
        second_bias,
        deconv_eight,
        eight_bias,
        lateral_four,
        lateral_eight,
        lateral_sixteen,
        lateral_thirty,
        lateral_gain,
        lateral_shift,
        smooth_weight,
        output_gain,
    ) = pyramid
    grads = [jnp.zeros(tensor.shape, wide_type) for tensor in pyramid]
    laterals = (lateral_four, lateral_eight, lateral_sixteen, lateral_thirty)
    if scale_level == 0:
        first_map = unfold_taps(apply_right(strip, deconv_first)) + first_bias.astype(wide_type)
        active, squash_pull = jax.vjp(
            squash, first_map, upnorm_gain.astype(wide_type), upnorm_shift.astype(wide_type)
        )
        active_low = active.astype(narrow_type)
        source = (
            unfold_taps(apply_left(active_low, deconv_second)) + second_bias.astype(wide_type)
        ).astype(narrow_type)
    elif scale_level == 1:
        source = (
            unfold_taps(apply_right(strip, deconv_eight)) + eight_bias.astype(wide_type)
        ).astype(narrow_type)
    elif scale_level == 2:
        source = strip
    else:
        images, row_count, col_count, channels = strip.shape
        pooled = jnp.mean(
            strip.astype(wide_type).reshape(images, row_count // 2, 2, col_count // 2, 2, channels),
            axis=(2, 4),
        )
        source = pooled.astype(narrow_type)
    source_grad, lateral_grad, gain_grad, shift_grad, smooth_grad, out_gain_grad = finish_level(
        source,
        laterals[scale_level],
        lateral_gain[scale_level],
        lateral_shift[scale_level],
        smooth_weight[scale_level],
        output_gain[scale_level],
        loss_weight,
        extend,
    )
    grads[8 + scale_level] = lateral_grad
    grads[12] = grads[12].at[scale_level].set(gain_grad)
    grads[13] = grads[13].at[scale_level].set(shift_grad)
    grads[14] = grads[14].at[scale_level].set(smooth_grad)
    grads[15] = grads[15].at[scale_level].set(out_gain_grad)
    if scale_level == 0:
        second_low = source_grad.astype(narrow_type)
        folded = fold_taps(second_low)
        grads[5] = position_sum(second_low)
        grads[4] = outer_sum(folded, active_low)
        active_grad = apply_right(folded, deconv_second)
        first_grad, grads[2], grads[3] = squash_pull(active_grad)
        first_low = first_grad.astype(narrow_type)
        folded = fold_taps(first_low)
        grads[1] = position_sum(first_low)
        grads[0] = outer_sum(strip, folded)
        strip_grad = apply_left(folded, deconv_first)
    elif scale_level == 1:
        eight_low = source_grad.astype(narrow_type)
        folded = fold_taps(eight_low)
        grads[7] = position_sum(eight_low)
        grads[6] = outer_sum(strip, folded)
        strip_grad = apply_left(folded, deconv_eight)
    elif scale_level == 2:
        strip_grad = source_grad
    else:
        images, row_count, col_count, channels = strip.shape
        spread_out = jnp.broadcast_to(
            source_grad[:, :, None, :, None, :] * 0.25,
            (images, row_count // 2, 2, col_count // 2, 2, channels),
        )
        strip_grad = spread_out.reshape(images, row_count, col_count, channels)
    return (strip_grad, tuple(grads))


def level_weight(scale_level, cotans, anchors, roi_mask):
    region = roi_mask
    if scale_level < 3:
        factor = (4, 2, 1)[scale_level]
        region = jnp.repeat(jnp.repeat(region, factor, axis=1), factor, axis=2)
    else:
        region = region[:, ::2, ::2]
    anchor = anchors[scale_level]
    cotangent = cotans[scale_level]
    return (anchor + region).astype(wide_type)[..., None] * cotangent.astype(wide_type)


def on_device(
    block_input,
    pre_gain,
    pre_shift,
    qkv_weight,
    qv_bias,
    rel_rows,
    rel_cols,
    proj_weight,
    proj_bias,
    mid_gain,
    mid_shift,
    fc1_weight,
    fc1_bias,
    fc2_weight,
    fc2_bias,
    deconv_first,
    first_bias,
    upnorm_gain,
    upnorm_shift,
    deconv_second,
    second_bias,
    deconv_eight,
    eight_bias,
    lateral_four,
    lateral_eight,
    lateral_sixteen,
    lateral_thirty,
    lateral_gain,
    lateral_shift,
    smooth_weight,
    output_gain,
    grad_four,
    grad_eight,
    grad_sixteen,
    grad_thirty,
    anchor_four,
    anchor_eight,
    anchor_sixteen,
    anchor_thirty,
    roi_mask,
):
    images, strip_rows, col_count, model_width = block_input.shape
    head_size = rel_rows.shape[1]
    head_count = model_width // head_size
    scale_factor = head_size ** (-0.5)
    height = strip_rows * lax.axis_size(("rows", "scale"))
    first_row = lax.axis_index(("rows", "scale")) * strip_rows
    pyramid = (
        deconv_first,
        first_bias,
        upnorm_gain,
        upnorm_shift,
        deconv_second,
        second_bias,
        deconv_eight,
        eight_bias,
        lateral_four,
        lateral_eight,
        lateral_sixteen,
        lateral_thirty,
        lateral_gain,
        lateral_shift,
        smooth_weight,
        output_gain,
    )
    cotans = (grad_four, grad_eight, grad_sixteen, grad_thirty)
    anchors = (anchor_four, anchor_eight, anchor_sixteen, anchor_thirty)
    inputs_wide = block_input.astype(wide_type)
    normed, pre_pull = jax.vjp(
        layer_norm, inputs_wide, pre_gain.astype(wide_type), pre_shift.astype(wide_type)
    )
    normed_low = normed.astype(narrow_type)
    mixed_all = apply_right(normed_low, qkv_weight)
    bias_wide = qv_bias.astype(wide_type)
    queries = (mixed_all[..., :model_width] + bias_wide[:model_width]).astype(narrow_type)
    keys_own = mixed_all[..., model_width : 2 * model_width].astype(narrow_type)
    values_own = (mixed_all[..., 2 * model_width :] + bias_wide[model_width:]).astype(narrow_type)
    keys_all, values_all = (
        lax.all_gather(keys_own, ("rows", "scale"), axis=1, tiled=True),
        lax.all_gather(values_own, ("rows", "scale"), axis=1, tiled=True),
    )
    row_wide = rel_rows.astype(wide_type)
    col_wide = rel_cols.astype(wide_type)
    row_hot = offset_hot(first_row, strip_rows, height, height)
    col_hot = offset_hot(0, col_count, col_count, col_count)
    row_table = offset_rows(row_hot, row_wide)
    col_table = offset_rows(col_hot, col_wide)
    query_heads = per_head(queries, head_count, head_size)
    key_heads = per_head(keys_all, head_count, head_size)
    value_heads = per_head(values_all, head_count, head_size)

    def attend_image(element):
        query_img, key_img, value_img = element
        scores = attention_scores(query_img, key_img, row_table, col_table)
        row_peak = jnp.max(scores, axis=-1, keepdims=True)
        exponent = jnp.exp(scores - row_peak)
        summed = jnp.sum(exponent, axis=-1, keepdims=True)
        weights = (exponent / summed).astype(narrow_type)
        mixed_out = jnp.einsum(
            "hqk,khc->qhc",
            weights,
            value_img.reshape(-1, head_count, head_size),
            preferred_element_type=wide_type,
        )
        return (mixed_out, (row_peak + jnp.log(summed))[..., 0])

    attended, log_norm = lax.map(attend_image, (query_heads, key_heads, value_heads))
    attended_low = attended.reshape(images, strip_rows, col_count, model_width).astype(narrow_type)
    branch = apply_right(attended_low, proj_weight) + proj_bias.astype(wide_type)
    middle = inputs_wide + branch
    normed_mid, mid_pull = jax.vjp(
        layer_norm, middle, mid_gain.astype(wide_type), mid_shift.astype(wide_type)
    )
    normed_mid_low = normed_mid.astype(narrow_type)
    hidden_pre = apply_right(normed_mid_low, fc1_weight) + fc1_bias.astype(wide_type)
    hidden_act, act_pull = jax.vjp(partial(jax.nn.gelu, approximate=False), hidden_pre)
    hidden_low = hidden_act.astype(narrow_type)
    result = middle + (apply_right(hidden_low, fc2_weight) + fc2_bias.astype(wide_type))
    result_low = result.astype(narrow_type)
    gathered = lax.all_gather(result_low, "scale", axis=1, tiled=True)

    def extend_rows(values):
        return padded_2(values, (("rows", 1),), 1)

    def owned_level(scale_level):

        def run_level(strip):
            weight = level_weight(scale_level, cotans, anchors, roi_mask)
            return pyramid_level(scale_level, extend_rows, strip, weight, pyramid)

        return run_level

    strip_grad, pyramid_grads = lax.switch(
        lax.axis_index("scale"), [owned_level(level_id) for level_id in range(4)], gathered
    )
    result_grad_wide = jax.tree.map(
        lambda part: part.astype(jnp.float32),
        lax.psum_scatter(as_sent(strip_grad), "scale", scatter_dimension=1, tiled=True),
    )
    result_grad = result_grad_wide.astype(narrow_type)
    fc2_bias_grad = position_sum(result_grad)
    (pre_act_grad,) = act_pull(apply_left(result_grad, fc2_weight))
    pre_low = pre_act_grad.astype(narrow_type)
    fc1_bias_grad = position_sum(pre_low)
    mid_grad, mid_gain_grad, mid_shift_grad = mid_pull(apply_left(pre_low, fc1_weight))
    middle_grad = result_grad.astype(wide_type) + mid_grad
    branch_low = middle_grad.astype(narrow_type)
    proj_bias_grad = position_sum(branch_low)
    attended_grad = apply_left(branch_low, proj_weight).astype(narrow_type)
    grad_heads = per_head(attended_grad, head_count, head_size)

    def query_pass(with_keys, element):
        query_img, grad_img, lse_img, key_img, value_img = element
        scores = attention_scores(query_img, key_img, row_table, col_table)
        weights = jnp.exp(scores - lse_img[..., None])
        grad_flat = grad_img.reshape(-1, head_count, head_size)
        key_flat = key_img.reshape(-1, head_count, head_size)
        prob_grad = jnp.einsum(
            "qhc,khc->hqk",
            grad_flat,
            value_img.reshape(-1, head_count, head_size),
            preferred_element_type=wide_type,
        )
        spread_sum = jnp.sum(weights * prob_grad, axis=-1)
        score_grad = (weights * (prob_grad - spread_sum[..., None])).astype(narrow_type)
        query_grad, row_part, col_part = score_back(
            score_grad, query_img, key_flat, row_table, col_table
        )
        query_flat = query_img.reshape(-1, head_count, head_size)
        key_grad = (
            jnp.einsum("hqk,qhc->khc", score_grad, query_flat, preferred_element_type=wide_type)
            * scale_factor
        )
        value_grad = jnp.einsum(
            "hqk,qhc->khc", weights.astype(narrow_type), grad_flat, preferred_element_type=wide_type
        )
        return (query_grad, row_part, col_part, spread_sum, key_grad, value_grad)

    query_grad, row_part, col_part, spread_sums, key_grad, value_grad = lax.map(
        partial(query_pass, True), (query_heads, grad_heads, log_norm, key_heads, value_heads)
    )
    full_shape = (images, height, col_count, model_width)
    key_part, value_part = (
        lax.psum_scatter(
            key_grad.reshape(full_shape).astype(jnp.bfloat16),
            ("rows", "scale"),
            scatter_dimension=1,
            tiled=True,
        ).astype(jnp.float32),
        lax.psum_scatter(
            value_grad.reshape(full_shape).astype(jnp.bfloat16),
            ("rows", "scale"),
            scatter_dimension=1,
            tiled=True,
        ).astype(jnp.float32),
    )
    rel_rows_grad = jnp.einsum("ijr,ijc->rc", row_hot, jnp.sum(row_part, axis=0), precision=highest)
    rel_cols_grad = jnp.einsum("ijr,ijc->rc", col_hot, jnp.sum(col_part, axis=0), precision=highest)
    query_low = query_grad.reshape(images, strip_rows, col_count, model_width).astype(narrow_type)
    key_low = key_part.astype(narrow_type)
    value_low = value_part.astype(narrow_type)
    joined_low = jnp.concatenate((query_low, key_low, value_low), axis=-1)
    qv_bias_grad = jnp.concatenate((position_sum(query_low), position_sum(value_low)))
    pre_in_grad, pre_gain_grad, pre_shift_grad = pre_pull(apply_left(joined_low, qkv_weight))
    input_grad = middle_grad + pre_in_grad
    pyramid_flat = (
        pyramid_grads[0].reshape(-1),
        pyramid_grads[4].reshape(-1),
        pyramid_grads[6].reshape(-1),
        pyramid_grads[8].reshape(-1),
        pyramid_grads[9].reshape(-1),
        pyramid_grads[10].reshape(-1),
        pyramid_grads[11].reshape(-1),
        pyramid_grads[14].reshape(-1),
    )
    flat_sums = lax.psum_scatter(
        (
            outer_sum(normed_low, joined_low).reshape(-1),
            outer_sum(attended_low, branch_low).reshape(-1),
            outer_sum(normed_mid_low, pre_low).reshape(-1),
            outer_sum(hidden_low, result_grad).reshape(-1),
        )
        + pyramid_flat,
        ("img", "rows", "scale"),
        scatter_dimension=0,
        tiled=True,
    )
    block_sums = flat_sums[:4]
    level_sums = flat_sums[4:]
    small_sums = lax.psum(
        (
            pre_gain_grad,
            pre_shift_grad,
            qv_bias_grad,
            rel_rows_grad,
            rel_cols_grad,
            proj_bias_grad,
            mid_gain_grad,
            mid_shift_grad,
            fc1_bias_grad,
            fc2_bias_grad,
            pyramid_grads[1],
            pyramid_grads[2],
            pyramid_grads[3],
            pyramid_grads[5],
            pyramid_grads[7],
            pyramid_grads[12],
            pyramid_grads[13],
            pyramid_grads[15],
        ),
        ("img", "rows", "scale"),
    )
    return (
        result_low,
        input_grad,
        small_sums[0],
        small_sums[1],
        block_sums[0],
        small_sums[2],
        small_sums[3],
        small_sums[4],
        block_sums[1],
        small_sums[5],
        small_sums[6],
        small_sums[7],
        block_sums[2],
        small_sums[8],
        block_sums[3],
        small_sums[9],
        level_sums[0],
        small_sums[10],
        small_sums[11],
        small_sums[12],
        level_sums[1],
        small_sums[13],
        level_sums[2],
        small_sums[14],
        level_sums[3],
        level_sums[4],
        level_sums[5],
        level_sums[6],
        small_sums[15],
        small_sums[16],
        level_sums[7],
        small_sums[17],
    )


def solution(mesh):
    in_specs = (
        P("img", ("rows", "scale"), None, None),
        P(),
        P(),
        P(),
        P(),
        P(),
        P(),
        P(),
        P(),
        P(),
        P(),
        P(),
        P(),
        P(),
        P(),
        P(),
        P(),
        P(),
        P(),
        P(),
        P(),
        P(),
        P(),
        P(),
        P(),
        P(),
        P(),
        P(),
        P(),
        P(),
        P(),
        P("img", "rows", None, None),
        P("img", "rows", None, None),
        P("img", "rows", None, None),
        P("img", "rows", None, None),
        P("img", "rows", None),
        P("img", "rows", None),
        P("img", "rows", None),
        P("img", "rows", None),
        P("img", "rows", None),
    )
    out_specs = (
        P("img", ("rows", "scale"), None, None),
        P("img", ("rows", "scale"), None, None),
        P(),
        P(),
        P(("img", "rows", "scale")),
        P(),
        P(),
        P(),
        P(("img", "rows", "scale")),
        P(),
        P(),
        P(),
        P(("img", "rows", "scale")),
        P(),
        P(("img", "rows", "scale")),
        P(),
        P(("img", "rows", "scale")),
        P(),
        P(),
        P(),
        P(("img", "rows", "scale")),
        P(),
        P(("img", "rows", "scale")),
        P(),
        P(("img", "rows", "scale")),
        P(("img", "rows", "scale")),
        P(("img", "rows", "scale")),
        P(("img", "rows", "scale")),
        P(),
        P(),
        P(("img", "rows", "scale")),
        P(),
    )
    return jax.shard_map(
        on_device, mesh=mesh, in_specs=in_specs, out_specs=out_specs, check_vma=False
    )
```

profile of v0, /device:TPU:1, one launch (start us, length us, event | category | flops | bytes accessed | tf_op | source)
XLA Modules:
  0.0 1784.0 jit_solution(8056181741418230613)
XLA Ops:
  38.5 22.6 %all-gather.5.cloned.1.call-done = bf16[1,16,64,768]{3,2,0,1:T(8,128)(2,1)} async-done(((bf16[1,2,64,768]{3,2,0,1:T(8,128)(2,1)}), bf16[1,16,64,768]{3,2,0,1:T(8,128)(2,1)}) %all-gather.5.cloned.1.call-update) | async-done | bytes 1572880 | tf_op jit(solution)/shard_map/all_gather | solution.py:361
  61.0 5.9 squeeze.42
  66.9 10.2 fusion.658
  77.1 13.3 copy.565
  91.1 7.3 exponential_reduce_fusion
  98.4 8.3 all-gather.3.cloned.1.call-done
  117.3 12.0 reshape.2516
  151.8 16.8 all_gather.11
  168.5 453.1 %conditional.1 = (bf16[1,8,64,768]{3,2,1,0:T(8,128)(2,1)}, f32[768,1536]{0,1:T(8,128)}, f32[384]{0:T(512)}, f32[384]{0:T(512)}, f32[384]{0:T(512)}, /*index=5*/f...) conditional(s32[]{:T(128)} %clamp.3, ...), branch_computations={%region_6.26_spmd, %region_26.39_spmd, %region_39.51_spmd, %region... | conditional | flops 39052660736 | bytes 1113164928 | solution.py:415
  179.9 7.8 fusion.55
  195.2 7.0 add_convert_fusion.4
  202.2 12.6 copy.519
  214.9 10.9 reshape.2394
  246.8 6.0 copy.509
  264.6 7.0 fusion.164
  282.7 11.0 copy.525
  293.7 8.2 convert_element_type.390
  305.7 5.6 fusion.51
  311.2 5.5 fusion.50
  322.2 5.5 fusion.48
  327.8 5.6 fusion.47
  333.3 5.5 fusion.79
  344.3 27.3 %fusion.656 = (f32[32,256]{1,0:T(8,128)}, f32[32,256,256]{2,1,0:T(8,128)}) fusion(bf16[4,2304,256]{2,1,0:T(8,128)(2,1)} %get-tuple-element.357, bf16[1,34,258,256]{3,2,1,0:T(8,128)(2,1)} %copy-done.3, f32[32,256,256]{2,1,0:T(8,128)} %fusion.79, f32[32,256,256]{2,1,0:T(8,128)} %fusion.51, f32[32,256,256]{2,1,0:T(8,128)} %fusion.50, ...), kind=kOutput, calls=%fused_computation.911 | convolution fusion | flops 1092608000 | bytes 79855616 | tf_op jit(solution)/shard_map/cond/branch_0_fun/...c,cn->...n/dot_general | solution.py:44
  383.8 8.5 fusion.1
  392.4 7.0 add_convert_fusion.1
  422.5 5.7 fusion.44
  440.5 5.6 fusion.16
  451.6 5.6 fusion.18
  462.6 5.5 fusion.12
  473.6 28.8 %multiply_reduce_fusion = (f32[256]{0:T(256)}, f32[32,256]{1,0:T(8,128)S(1)}, f32[256]{0:T(256)}, f32[32,256,256]{2,1,0:T(8,128)}) fusion(f32[32,256,256]{2,1,0:T(8,128)} %copy-done.1, f32[32,256]{1,0:T(8,128)S(1)} %copy-done.56, f32[32,256]{1,0:T(8,128)S(1)} %copy-done.54, f32[256]{0:T(256)S(1)} %bitcast.1313, ...), kind=kOutput, calls=%fused_computation.9 | convolution fusion | flops 1107287552 | bytes 88312832 | tf_op jit(solution)/shard_map/cond/branch_0_fun/...c,nc->...n/dot_general | solution.py:48
  502.4 7.6 fusion.637
  515.0 6.1 copy.521
  521.1 7.4 reshape.2412
  528.6 10.8 copy.522
  539.4 12.7 fusion.632
  622.4 22.4 %reduce-scatter.4.cloned.1.call-done = bf16[1,2,64,768]{3,2,1,0:T(8,128)(2,1)} async-done(((bf16[1,8,64,768]{3,2,1,0:T(8,128)(2,1)}), bf16[1,2,64,768]{3,2,1,0:T(8,128)(2,1)}) %reduce-scatter.4.cloned.1.call-update) | async-done | bytes 196624 | tf_op jit(solution)/shard_map/reduce_scatter | solution.py:420
  644.9 5.9 convert_reduce_fusion.3
  713.8 6.1 copy.590
  719.9 5.6 reshape.2529
  727.9 5.7 reshape.2531
  743.1 14.6 copy.666
  757.6 9.5 reshape.2551
  776.5 9.3 fusion.633
  804.1 5.8 copy.665
  815.0 10.8 reshape.2528
  831.1 7.9 reshape.2525
  862.0 732.0 %all-reduce.43.cloned.1.call-done = (f32[1769472]{0:T(1024)}, f32[589824]{0:T(1024)}, f32[2359296]{0:T(1024)}, f32[2359296]{0:T(1024)}, f32[1179648]{0:T(1024)},...) async-done(((f32[1769472]{0:T(1024)}, f32[589824]{0:T(1024)}, ...) | async-done | bytes 50528272
  1612.2 141.8 %all-reduce.41.cloned.1.call-done = (f32[768]{0:T(1024)}, f32[768]{0:T(1024)}, f32[1536]{0:T(1024)}, f32[31,64]{1,0:T(8,128)}, f32[127,64]{0,1:T(8,128)}, /*inde...) async-done(((f32[768]{0:T(1024)}, f32[768]{0:T(1024)}, ...) | async-done | bytes 96528 | tf_op jit(solution)/shard_map/psum | solution.py:512
  (459 shorter events, 428.2 us)
Async XLA Ops:
  7.2 53.8 %all-gather.5.cloned.1.call-start = ((), (), s32[]{:S(2)}) async-start(), calls=%async_computation.4 | async-start | bytes 1769472 | tf_op jit(solution)/shard_map/all_gather | solution.py:361
  11.8 10.2 copy-start.113
  15.2 91.5 %all-gather.3.cloned.1.call-start = ((), (), s32[]{:S(2)}) async-start(), calls=%async_computation.3 | async-start | bytes 1769472 | tf_op jit(solution)/shard_map/all_gather | solution.py:362
  18.0 626.9 %reduce-scatter.4.cloned.1.call-start = ((), (), s32[]{:S(2)}) async-start(), calls=%async_computation.5 | async-start | bytes 983040 | tf_op jit(solution)/shard_map/reduce_scatter | solution.py:420
  24.7 7.0 copy-start.142
  24.7 7.6 copy-start.143
  32.3 109.4 %copy-start.75 = (f32[768]{0:T(1024)}, f32[768]{0:T(1024)S(1)}, u32[]{:S(2)}) copy-start(f32[768]{0:T(1024)S(1)} %convert_element_type.486) | copy-start | bytes 9220
  117.3 12.1 copy-start.101
  130.1 9.0 copy-start.115
  140.9 9.3 copy-start.19
  141.7 8.5 slice-start.6
  141.7 8.4 slice-start.7
  150.2 18.3 %copy-start.144 = (bf16[384]{0:T(512)(128)(2,1)S(1)}, bf16[384]{0:T(512)(128)(2,1)}, u32[]{:S(2)}) copy-start(bf16[384]{0:T(512)(128)(2,1)} %param.92) | copy-start | bytes 2308
  150.2 18.3 %copy-start.145 = (bf16[384]{0:T(512)(128)(2,1)S(1)}, bf16[384]{0:T(512)(128)(2,1)}, u32[]{:S(2)}) copy-start(bf16[384]{0:T(512)(128)(2,1)} %param.93) | copy-start | bytes 2308
  169.1 7.9 copy-start.94
  239.1 62.9 %collective-permute-start.9 = (bf16[1,1,256,256]{3,2,1,0:T(8,128)(2,1)}, bf16[1,1,256,256]{3,2,1,0:T(8,128)(2,1)}, u32[]{:S(2)}, u32[]{:S(2)}) collective-permute-start(bf16[1,1,256,256]{3,2,1,0:T(8,128)(2,1)} %get-tuple-element.1202), channel_id=1, source_target_pairs={{4,0},{5,1},{6,2},{7,3},{12,8},{13,9},{14,10},{15,11},{20,16},{21,... | collective-permute-start | bytes 393224 | tf_op jit(solution)/shard_map/cond/branch_0_fun/ppermute | solution.py:22
  240.4 61.6 %collective-permute-start.8 = (bf16[1,1,256,256]{3,2,1,0:T(8,128)(2,1)}, bf16[1,1,256,256]{3,2,1,0:T(8,128)(2,1)}, u32[]{:S(2)}, u32[]{:S(2)}) collective-permute-start(bf16[1,1,256,256]{3,2,1,0:T(8,128)(2,1)} %get-tuple-element.1201), channel_id=1, source_target_pairs={{0,4},{1,5},{2,6},{3,7},{8,12},{9,13},{10,14},{11,15},{16,20},{17,... | collective-permute-start | bytes 393224 | tf_op jit(solution)/shard_map/cond/branch_0_fun/ppermute | solution.py:21
  264.6 15.1 copy-start.89
  282.1 11.6 copy-start.81
  293.7 8.3 copy-start.128
  305.7 22.1 %copy-start.3 = (bf16[1,34,258,256]{3,2,1,0:T(8,128)(2,1)}, bf16[1,34,258,256]{3,2,1,0:T(8,128)(2,1)S(1)}, u32[]{:S(2)}) copy-start(bf16[1,34,258,256]{3,2,1,0:T(8,128)(2,1)S(1)} %fusion.8) | copy-start | bytes 13473796 | tf_op jit(solution)/shard_map/cond
  383.8 15.6 slice-start.2
  392.4 7.0 slice-start.3
  399.4 7.0 copy-start.9
  400.7 32.5 %collective-permute-start.11 = (bf16[1,1,256,256]{3,2,1,0:T(8,128)(2,1)S(1)}, bf16[1,1,256,256]{3,2,1,0:T(8,128)(2,1)S(1)}, u32[]{:S(2)}, u32[]{:S(2)}) collective-permute-start(bf16[1,1,256,256]{3,2,1,0:T(8,128)(2,1)S(1)} %get-tuple-element.1199), channel_id=1, source_target_pairs={{4,0},{5,1},{6,2},{7,3},{12,8},{13,9},{14,10},{15,11},{20,16},{21,... | collective-permute-start | bytes 393224 | tf_op jit(solution)/shard_map/cond/branch_0_fun/ppermute | solution.py:22
  402.0 31.2 %collective-permute-start.10 = (bf16[1,1,256,256]{3,2,1,0:T(8,128)(2,1)S(1)}, bf16[1,1,256,256]{3,2,1,0:T(8,128)(2,1)S(1)}, u32[]{:S(2)}, u32[]{:S(2)}) collective-permute-start(bf16[1,1,256,256]{3,2,1,0:T(8,128)(2,1)S(1)} %get-tuple-element.1200), channel_id=1, source_target_pairs={{0,4},{1,5},{2,6},{3,7},{8,12},{9,13},{10,14},{11,15},{16,20},{17,... | collective-permute-start | bytes 393224 | tf_op jit(solution)/shard_map/cond/branch_0_fun/ppermute | solution.py:21
  473.6 28.8 %copy-start.74 = (f32[32,256]{1,0:T(8,128)S(1)}, f32[32,256]{1,0:T(8,128)}, u32[]{:S(2)}) copy-start(f32[32,256]{1,0:T(8,128)} %copy-done.73) | copy-start | bytes 98308 | tf_op jit(solution)/shard_map/cond
  502.4 7.7 copy-start.66
  528.6 10.8 copy-start.85
  528.6 10.8 copy-start.86
  539.4 12.7 copy-start.82
  539.4 12.7 copy-start.13
  539.4 12.7 copy-start.96
  539.4 12.7 copy-start.106
  570.6 11.3 slice-start.4
  621.7 204.1 %reduce-scatter.8.cloned.1.call-start = ((), (), s32[]{:S(2)}) async-start(), calls=%async_computation.7 | async-start | bytes 1769472 | tf_op jit(solution)/shard_map/reduce_scatter | solution.py:472
  676.3 149.5 %reduce-scatter.6.cloned.1.call-start = ((), (), s32[]{:S(2)}) async-start(), calls=%async_computation.6 | async-start | bytes 1769472 | tf_op jit(solution)/shard_map/reduce_scatter | solution.py:466
  702.8 891.3 %all-reduce.43.cloned.1.call-start = ((), (), s32[]{:S(2)}) async-start(), calls=%async_computation.9 | async-start | bytes 101056512
  815.0 10.8 copy-start.65
  815.0 10.8 copy-start.68
  815.0 10.8 copy-start.91
  815.0 10.8 copy-start.93
  839.0 915.0 %all-reduce.41.cloned.1.call-start = ((), (), s32[]{:S(2)}) async-start(), calls=%async_computation.8 | async-start | bytes 231424 | tf_op jit(solution)/shard_map/psum | solution.py:512
  841.5 7.0 copy-start.70
  843.5 7.1 copy-start.21
  843.5 7.1 copy-start.60
  843.5 7.1 copy-start.61
  843.5 7.1 copy-start.77
  (78 other events, 274.0 us)
Sparse Core Ops, SparseCore 0:
  15.3 45.6 all-gather.4
  63.7 42.9 all-gather.2
  621.8 23.0 reduce-scatter.3
  676.4 64.2 reduce-scatter.7
  744.4 63.8 reduce-scatter.5
  839.1 754.8 all-reduce.42
  1602.8 151.2 all-reduce.40
where the time goes:
time: 1800 us; the launch traced here: 1780 us
  waiting for transfers between devices  927 us (52%)
  local copies, waits for them, and re-layouts  369 us (20%)
  matrix products  303 us (17%)
  other arithmetic  110 us (6%)
  loops' own time  30.1 us (2%)
    unnamed x8, waiting for transfers between devices  732 us
    psum x1, waiting for transfers between devices, on_device(): lax.psum((pre_gain_grad, pre_shift_grad, qv_bias_grad, rel_rows_grad, rel...  142 us
    dot_general x16, matrix products, apply_right(): jnp.einsum('...c,cn->...n', values, weight, preferred_element_type=wide_t...  102 us
    dot_general x16, matrix products, apply_left(): jnp.einsum('...c,nc->...n', values, weight, preferred_element_type=wide_t...  101 us
    unnamed x156, local copies, waits for them, and re-layouts  70.8 us
    dot_general x16, matrix products, outer_sum(): jnp.einsum('...a,...b->ab', left_side, right_side, preferred_element_type...  43.1 us
  transfers between devices with their start and end apart: 11, of which 5 were waited for; matrix products, arithmetic and copies ran while one was open for 18% of the time, Pallas kernels for 0%

commit v1 on v0

--- a/solution.py
+++ b/solution.py
@@ -3,6 +3,8 @@
 import jax
 import jax.numpy as jnp
 from jax import lax
+from jax.experimental import pallas as pl
+from jax.experimental.pallas import tpu as pltpu
 from jax.sharding import PartitionSpec as P
 
 highest = lax.Precision.HIGHEST
@@ -10,18 +12,263 @@
 wide_type = jnp.float32
 narrow_type = jnp.bfloat16
 
-
-def padded_2(value, sides, width):
-    for axis, dim in sides:
-        size, length = (lax.axis_size(axis), value.shape[dim])
-        up = [(i, (i + 1) % size) for i in range(size - 1)]
-        down = [(j, i) for i, j in up]
-        last = lax.slice_in_dim(value, length - width, length, axis=dim)
-        initial = lax.slice_in_dim(value, 0, width, axis=dim)
-        before = lax.ppermute(last, axis, up)
-        after = lax.ppermute(initial, axis, down)
-        value = jnp.concatenate([before, value, after], axis=dim)
-    return value
+MESH_ID = pl.DeviceIdType.MESH
+lanes = 128
+
+
+def axis_bits(size):
+    bits = []
+    step = 1
+    while step < size:
+        bits.append(step)
+        step *= 2
+    return bits
+
+
+def bit_partner(axis, step):
+    here = lax.axis_index(axis)
+    bit = lax.rem(lax.div(here, step), 2)
+    return {axis: here + step - 2 * step * bit}, bit
+
+
+def reduce_kernel(orders, dims, stages, refs):
+    count = len(orders)
+    sources = refs[:count]
+    small_in = refs[count]
+    outs = refs[count + 1 : 2 * count + 1]
+    small_out = refs[2 * count + 1]
+    scratch = refs[2 * count + 2 :]
+    held = scratch[:count]
+    landed = [scratch[count + t * stages : count + (t + 1) * stages] for t in range(count)]
+    rest = scratch[count + count * stages :]
+    small_held, small_landed = rest[0], rest[1]
+    send_sem, recv_sem, local_sem, small_send, small_recv = rest[2:]
+    partners = [bit_partner(axis, step) for axis, step in dims]
+    barrier = pltpu.get_barrier_semaphore()
+    for partner, _ in partners:
+        pl.semaphore_signal(barrier, inc=1, device_id=partner, device_id_type=MESH_ID)
+    pl.semaphore_wait(barrier, len(dims))
+
+    def picked(taken, current, keep):
+        index = []
+        for dim in range(len(dims)):
+            bit = partners[dim][1]
+            if dim in taken:
+                index.append(bit)
+            elif dim == current:
+                index.append(bit if keep else 1 - bit)
+            else:
+                index.append(slice(None))
+        return index
+
+    def held_index(index):
+        core = core_dim(dims)
+        return tuple(index[:core] + index[core + 1 :])
+
+    def copy(t, stage):
+        current = orders[t][stage]
+        taken = set(orders[t][:stage])
+        index = picked(taken, current, False)
+        if stage == 0:
+            source = sources[t].at[tuple(index)]
+        else:
+            source = held[t].at[held_index(index)]
+        return pltpu.make_async_remote_copy(
+            src_ref=source,
+            dst_ref=landed[t][stage],
+            send_sem=send_sem.at[t, stage],
+            recv_sem=recv_sem.at[t, stage],
+            device_id=partners[current][0],
+            device_id_type=MESH_ID,
+        )
+
+    def local_copy(t):
+        index = picked(set(), orders[t][0], True)
+        return pltpu.make_async_copy(sources[t].at[tuple(index)], held[t], local_sem.at[t])
+
+    def add(t, stage):
+        current = orders[t][stage]
+        taken = set(orders[t][:stage])
+        index = held_index(picked(taken, current, True))
+        target = held[t].at[index]
+        arrived = landed[t][stage]
+        lead = arrived.shape[:-2]
+        rows = arrived.shape[-2]
+        total = 1
+        for size in lead:
+            total *= size
+        def body(step, carry):
+            place = []
+            rem_step = step
+            for size in reversed(lead):
+                place.append(lax.rem(rem_step, size))
+                rem_step = lax.div(rem_step, size)
+            place = tuple(reversed(place))
+            target[place] = target[place] + arrived[place]
+            return carry
+
+        if lead:
+            lax.fori_loop(0, total, body, 0)
+        else:
+            target[...] = target[...] + arrived[...]
+
+    def small_copy(stage):
+        return pltpu.make_async_remote_copy(
+            src_ref=small_held,
+            dst_ref=small_landed.at[stage],
+            send_sem=small_send.at[stage],
+            recv_sem=small_recv.at[stage],
+            device_id=partners[orders[0][stage]][0],
+            device_id_type=MESH_ID,
+        )
+
+    small_held[...] = small_in[...]
+    small_copy(0).start()
+    for t in range(count):
+        copy(t, 0).start()
+        local_copy(t).start()
+    for stage in range(stages):
+        for t in range(count):
+            copy(t, stage).wait_recv()
+            if stage == 0:
+                local_copy(t).wait()
+            add(t, stage)
+            if stage + 1 < stages:
+                copy(t, stage + 1).start()
+            else:
+                index = held_index(picked(set(orders[t]), -1, True))
+                outs[t][...] = held[t][index].astype(jnp.float32)
+        small_copy(stage).wait()
+        small_held[...] = small_held[...] + small_landed[stage]
+        if stage + 1 < stages:
+            small_copy(stage + 1).start()
+    small_out[...] = small_held[...]
+    for t in range(count):
+        for stage in range(stages):
+            copy(t, stage).wait_send()
+
+
+def core_dim(dims):
+    return [i for i, (axis, step) in enumerate(dims) if axis == "img" and step == 1][0]
+
+
+def reduce_all(pieces, small, call_id):
+    sizes = {axis: lax.axis_size(axis) for axis in ("img", "rows", "scale")}
+    dims = []
+    for axis in ("img", "rows", "scale"):
+        for step in reversed(axis_bits(sizes[axis])):
+            dims.append((axis, step))
+    core = core_dim(dims)
+    plane = [i for i, (axis, step) in enumerate(dims) if axis == "img" and i != core]
+    across = [i for i, (axis, step) in enumerate(dims) if axis == "rows"]
+    along = list(reversed([i for i, (axis, step) in enumerate(dims) if axis == "scale"]))
+    first_order = [core] + across + plane + along
+    second_order = [core] + plane + across + along
+    count, stages = len(pieces), len(dims)
+    orders = [first_order if t % 2 == 0 else second_order for t in range(count)]
+    shapes = [piece.shape[1:] for piece in pieces]
+    shaped = [piece.reshape((2,) * stages + piece.shape[1:]) for piece in pieces]
+    scratch = [pltpu.VMEM((2,) * (stages - 1) + shape, jnp.bfloat16) for shape in shapes]
+    for t in range(count):
+        for stage in range(stages):
+            scratch.append(pltpu.VMEM((2,) * (stages - 1 - stage) + shapes[t], jnp.bfloat16))
+    scratch += [
+        pltpu.VMEM(small.shape, jnp.float32),
+        pltpu.VMEM((stages,) + small.shape, jnp.float32),
+        pltpu.SemaphoreType.DMA((count, stages)),
+        pltpu.SemaphoreType.DMA((count, stages)),
+        pltpu.SemaphoreType.DMA((count,)),
+        pltpu.SemaphoreType.DMA((stages,)),
+        pltpu.SemaphoreType.DMA((stages,)),
+    ]
+
+    def body(*refs):
+        reduce_kernel(orders, dims, stages, refs)
+
+    vmem = pl.BlockSpec(memory_space=pltpu.VMEM)
+    got = pl.pallas_call(
+        body,
+        out_shape=[jax.ShapeDtypeStruct(shape, jnp.float32) for shape in shapes]
+        + [jax.ShapeDtypeStruct(small.shape, jnp.float32)],
+        in_specs=[pl.BlockSpec(memory_space=pl.ANY)] * count + [vmem],
+        out_specs=[vmem] * (count + 1),
+        scratch_shapes=scratch,
+        compiler_params=pltpu.CompilerParams(
+            collective_id=call_id, has_side_effects=True, vmem_limit_bytes=62 << 20
+        ),
+        name="reduce_grads",
+    )(*shaped, small)
+    return got[:-1], got[-1]
+
+
+def pack_small(parts):
+    flat = jnp.concatenate([part.reshape(-1) for part in parts])
+    unit = 8 * lanes
+    total = -(-flat.shape[0] // unit) * unit
+    return jnp.pad(flat, (0, total - flat.shape[0])).reshape(-1, lanes)
+
+
+def unpack_small(packed, parts):
+    flat = packed.reshape(-1)
+    out, at = [], 0
+    for part in parts:
+        out.append(flat[at : at + part.size].reshape(part.shape))
+        at += part.size
+    return out
+
+
+def chunk_piece(parts):
+    stacked = jnp.concatenate(parts, axis=1) if len(parts) > 1 else parts[0]
+    rows = stacked.shape[1]
+    extra = -rows % 16
+    if extra:
+        stacked = jnp.pad(stacked, ((0, 0), (0, extra), (0, 0)))
+    return stacked
+
+
+def reduce_weights(groups, small_parts, call_id):
+    devices = lax.axis_size(("img", "rows", "scale"))
+    pieces, plans = [], []
+    for group in groups:
+        cut, plan = [], []
+        for grad in group:
+            rows, columns = grad.shape
+            own = rows // devices
+            chunk = grad.astype(narrow_type).reshape(devices, own, columns)
+            folds = 1
+            while (own * folds) % 16 and columns % (2 * folds * lanes) == 0:
+                folds *= 2
+            width = columns // folds
+            if folds > 1:
+                cut += [chunk[:, :, f * width : (f + 1) * width] for f in range(folds)]
+            else:
+                cut.append(chunk)
+            plan.append((own, columns, folds))
+        pieces.append(chunk_piece(cut))
+        plans.append(plan)
+    sums, small = reduce_all(pieces, pack_small(small_parts), call_id)
+    out = []
+    for plan, summed in zip(plans, sums):
+        at, got = 0, []
+        for own, columns, folds in plan:
+            parts = []
+            for f in range(folds):
+                parts.append(summed[at : at + own])
+                at += own
+            whole = jnp.concatenate(parts, axis=1) if folds > 1 else parts[0]
+            got.append(whole.reshape(-1))
+        out.append(got)
+    return out, unpack_small(small, small_parts)
+
+
+def with_edges(value):
+    axes = ("rows", "scale")
+    size, length = (lax.axis_size(axes), value.shape[1])
+    up = [(i, i + 1) for i in range(size - 1)]
+    down = [(j, i) for i, j in up]
+    before = lax.ppermute(value[:, length - 1 :], axes, up)
+    after = lax.ppermute(value[:, :1], axes, down)
+    return jnp.concatenate([before, value, after], axis=1)
 
 
 def as_sent(value):
@@ -125,49 +372,55 @@
     return (plain_part + rel_part, row_part, col_part)
 
 
-def smooth_forward(values, weight, extend):
-    row_count, col_count, channels = (values.shape[1], values.shape[2], values.shape[3])
-    padded = jnp.pad(extend(values), ((0, 0), (0, 0), (1, 1), (0, 0)))
-    summed = jnp.zeros(values.shape[:3] + (weight.shape[1],), wide_type)
-    for offset_tap in range(9):
-        row_step, col_step = (offset_tap // 3, offset_tap % 3)
-        window = padded[:, row_step : row_step + row_count, col_step : col_step + col_count]
-        summed = summed + apply_right(
-            window, weight[offset_tap * channels : (offset_tap + 1) * channels]
-        )
+def smooth_forward(values, weight):
+    padded = with_edges(values)
+    channels = values.shape[-1]
+    kernel = weight.reshape(3, 3, channels, weight.shape[1])
+    summed = lax.conv_general_dilated(
+        padded,
+        kernel,
+        (1, 1),
+        ((0, 0), (1, 1)),
+        dimension_numbers=("NHWC", "HWIO", "NHWC"),
+        preferred_element_type=wide_type,
+    )
     return (summed, padded)
 
 
-def smooth_backward(padded, upstream, weight, extend):
-    row_count, col_count = (upstream.shape[1], upstream.shape[2])
-    channels = padded.shape[3]
-    beside_all = jnp.pad(extend(upstream), ((0, 0), (0, 0), (1, 1), (0, 0)))
-    input_grad = jnp.zeros(upstream.shape[:3] + (channels,), wide_type)
-    pieces = []
-    for offset_tap in range(9):
-        row_step, col_step = (offset_tap // 3, offset_tap % 3)
-        window = padded[:, row_step : row_step + row_count, col_step : col_step + col_count]
-        pieces.append(outer_sum(window, upstream))
-        back_window = beside_all[
-            :, 2 - row_step : 2 - row_step + row_count, 2 - col_step : 2 - col_step + col_count
-        ]
-        input_grad = input_grad + apply_left(
-            back_window, weight[offset_tap * channels : (offset_tap + 1) * channels]
-        )
-    return (input_grad, jnp.concatenate(pieces, axis=0))
-
-
-def finish_level(source, lateral, gain_vec, shift_vec, smooth, out_gain, loss_weight, extend):
+def smooth_backward(padded, upstream, weight):
+    channels, outputs = padded.shape[3], upstream.shape[3]
+    beside_all = with_edges(upstream)
+    kernel = weight.reshape(3, 3, channels, outputs)[::-1, ::-1]
+    input_grad = lax.conv_general_dilated(
+        beside_all,
+        kernel,
+        (1, 1),
+        ((0, 0), (1, 1)),
+        dimension_numbers=("NHWC", "HWOI", "NHWC"),
+        preferred_element_type=wide_type,
+    )
+    weight_grad = lax.conv_general_dilated(
+        padded,
+        upstream,
+        (1, 1),
+        ((0, 0), (1, 1)),
+        dimension_numbers=("CHWN", "IHWO", "HWNC"),
+        preferred_element_type=wide_type,
+    )
+    return (input_grad, weight_grad.reshape(9 * channels, outputs))
+
+
+def finish_level(source, lateral, gain_vec, shift_vec, smooth, out_gain, loss_weight):
     reduced = apply_left(source, lateral)
     normed, norm_pull = jax.vjp(
         layer_norm, reduced, gain_vec.astype(wide_type), shift_vec.astype(wide_type)
     )
     normed_low = normed.astype(narrow_type)
-    smoothed, padded = smooth_forward(normed_low, smooth, extend)
+    smoothed, padded = smooth_forward(normed_low, smooth)
     level_out, out_pull = jax.vjp(scaled_norm, smoothed, out_gain.astype(wide_type))
     smoothed_grad, out_gain_grad = out_pull(loss_weight)
     smoothed_low = smoothed_grad.astype(narrow_type)
-    normed_grad, smooth_grad = smooth_backward(padded, smoothed_low, smooth, extend)
+    normed_grad, smooth_grad = smooth_backward(padded, smoothed_low, smooth)
     reduced_grad, gain_grad, shift_grad = norm_pull(normed_grad)
     reduced_low = reduced_grad.astype(narrow_type)
     lateral_grad = outer_sum(reduced_low, source)
@@ -179,7 +432,7 @@
     return jax.nn.gelu(layer_norm(pre_values, gain_vec, shift_vec), approximate=False)
 
 
-def pyramid_level(scale_level, extend, strip, loss_weight, pyramid):
+def pyramid_level(scale_level, strip, loss_weight, pyramid):
     (
         deconv_first,
         first_bias,
@@ -230,7 +483,6 @@
         smooth_weight[scale_level],
         output_gain[scale_level],
         loss_weight,
-        extend,
     )
     grads[8 + scale_level] = lateral_grad
     grads[12] = grads[12].at[scale_level].set(gain_grad)
@@ -267,15 +519,21 @@
     return (strip_grad, tuple(grads))
 
 
-def level_weight(scale_level, cotans, anchors, roi_mask):
-    region = roi_mask
+def own_rows(values, count):
+    return lax.dynamic_slice_in_dim(values, lax.axis_index("scale") * count, count, axis=1)
+
+
+def level_weight(scale_level, strip_rows, cotans, anchors, roi_mask):
+    region = own_rows(roi_mask, strip_rows)
     if scale_level < 3:
         factor = (4, 2, 1)[scale_level]
         region = jnp.repeat(jnp.repeat(region, factor, axis=1), factor, axis=2)
+        count = factor * strip_rows
     else:
         region = region[:, ::2, ::2]
-    anchor = anchors[scale_level]
-    cotangent = cotans[scale_level]
+        count = strip_rows // 2
+    anchor = own_rows(anchors[scale_level], count)
+    cotangent = own_rows(cotans[scale_level], count)
     return (anchor + region).astype(wide_type)[..., None] * cotangent.astype(wide_type)
 
 
@@ -399,27 +657,14 @@
     hidden_low = hidden_act.astype(narrow_type)
     result = middle + (apply_right(hidden_low, fc2_weight) + fc2_bias.astype(wide_type))
     result_low = result.astype(narrow_type)
-    gathered = lax.all_gather(result_low, "scale", axis=1, tiled=True)
-
-    def extend_rows(values):
-        return padded_2(values, (("rows", 1),), 1)
-
-    def owned_level(scale_level):
-
-        def run_level(strip):
-            weight = level_weight(scale_level, cotans, anchors, roi_mask)
-            return pyramid_level(scale_level, extend_rows, strip, weight, pyramid)
-
-        return run_level
-
-    strip_grad, pyramid_grads = lax.switch(
-        lax.axis_index("scale"), [owned_level(level_id) for level_id in range(4)], gathered
-    )
-    result_grad_wide = jax.tree.map(
-        lambda part: part.astype(jnp.float32),
-        lax.psum_scatter(as_sent(strip_grad), "scale", scatter_dimension=1, tiled=True),
-    )
-    result_grad = result_grad_wide.astype(narrow_type)
+    strip_grad = 0.0
+    pyramid_grads = [jnp.zeros(tensor.shape, wide_type) for tensor in pyramid]
+    for scale_level in range(4):
+        weight = level_weight(scale_level, strip_rows, cotans, anchors, roi_mask)
+        level_strip, level_grads = pyramid_level(scale_level, result_low, weight, pyramid)
+        strip_grad = strip_grad + level_strip
+        pyramid_grads = [held + grad for held, grad in zip(pyramid_grads, level_grads)]
+    result_grad = strip_grad.astype(narrow_type)
     fc2_bias_grad = position_sum(result_grad)
     (pre_act_grad,) = act_pull(apply_left(result_grad, fc2_weight))
     pre_low = pre_act_grad.astype(narrow_type)
@@ -485,31 +730,24 @@
     qv_bias_grad = jnp.concatenate((position_sum(query_low), position_sum(value_low)))
     pre_in_grad, pre_gain_grad, pre_shift_grad = pre_pull(apply_left(joined_low, qkv_weight))
     input_grad = middle_grad + pre_in_grad
-    pyramid_flat = (
-        pyramid_grads[0].reshape(-1),
-        pyramid_grads[4].reshape(-1),
-        pyramid_grads[6].reshape(-1),
-        pyramid_grads[8].reshape(-1),
-        pyramid_grads[9].reshape(-1),
-        pyramid_grads[10].reshape(-1),
-        pyramid_grads[11].reshape(-1),
-        pyramid_grads[14].reshape(-1),
-    )
-    flat_sums = lax.psum_scatter(
-        (
-            outer_sum(normed_low, joined_low).reshape(-1),
-            outer_sum(attended_low, branch_low).reshape(-1),
-            outer_sum(normed_mid_low, pre_low).reshape(-1),
-            outer_sum(hidden_low, result_grad).reshape(-1),
-        )
-        + pyramid_flat,
-        ("img", "rows", "scale"),
-        scatter_dimension=0,
-        tiled=True,
-    )
-    block_sums = flat_sums[:4]
-    level_sums = flat_sums[4:]
-    small_sums = lax.psum(
+    smooth_grad = pyramid_grads[14].reshape(-1, pyramid_grads[14].shape[-1])
+    groups = [
+        [smooth_grad],
+        [pyramid_grads[0], pyramid_grads[6]],
+        [outer_sum(normed_mid_low, pre_low)],
+        [outer_sum(hidden_low, result_grad)],
+        [outer_sum(normed_low, joined_low)],
+        [
+            outer_sum(attended_low, branch_low),
+            pyramid_grads[4],
+            pyramid_grads[10],
+            pyramid_grads[11],
+            pyramid_grads[9],
+        ],
+        [pyramid_grads[8]],
+    ]
+    group_sums, small_sums = reduce_weights(
+        groups,
         (
             pre_gain_grad,
             pre_shift_grad,
@@ -530,7 +768,18 @@
             pyramid_grads[13],
             pyramid_grads[15],
         ),
-        ("img", "rows", "scale"),
+        0,
+    )
+    block_sums = (group_sums[4][0], group_sums[5][0], group_sums[2][0], group_sums[3][0])
+    level_sums = (
+        group_sums[1][0],
+        group_sums[5][1],
+        group_sums[1][1],
+        group_sums[6][0],
+        group_sums[5][4],
+        group_sums[5][2],
+        group_sums[5][3],
+        group_sums[0][0],
     )
     return (
         result_low,

time: 1800 us -> 927 us (0.52)
  waiting for transfers between devices: 927 us -> 68.3 us
  Pallas kernels: 0 us -> 159 us
  local copies, waits for them, and re-layouts: 369 us -> 217 us
  matrix products: 303 us -> 185 us
  other arithmetic: 110 us -> 215 us
  starting transfers between devices: 12.8 us -> 51.3 us
  loops' own time: 30.1 us -> 0 us
    unnamed x8 -> x4, waiting for transfers between devices: 732 us -> 0.07 us
    pallas_call x0 -> x1, Pallas kernels: none -> 159 us  [reduce_all(): pl.pallas_call(body, out_shape=[jax.ShapeDtypeStruct(shape, jnp.float32)...]
    psum x1 -> x0, waiting for transfers between devices: 142 us -> none  [on_device(): lax.psum((pre_gain_grad, pre_shift_grad, qv_bias_grad, rel_rows_grad, rel...]
    dot_general x16 -> x11, matrix products: 102 us -> 19.6 us  [apply_right(): jnp.einsum('...c,cn->...n', values, weight, preferred_element_type=wide_t...]
    conv_general_dilated x0 -> x12, matrix products: none -> 80 us  [the longest x4 27.7 us: smooth_forward(): lax.conv_general_dilated(padded, kernel, (1, 1), ((0, 0), (1, 1)), dimens...]
    dot_general x16 -> x11, matrix products: 101 us -> 24.8 us  [apply_left(): jnp.einsum('...c,nc->...n', values, weight, preferred_element_type=wide_t...]
    reduce_scatter x1, waiting for transfers between devices: 0.01 us -> 55 us  [on_device(): lax.psum_scatter(key_grad.reshape(full_shape).astype(jnp.bfloat16), ('row...]
    unnamed x156 -> x497, local copies, waits for them, and re-layouts: 70.8 us -> 22 us
  transfers between devices with their start and end apart: 11 -> 20, of which waited for: 5 -> 3; matrix products, arithmetic and copies ran while one was open for 18% -> 47% of each run, Pallas kernels for 0% -> 0%
where the time goes in v1:
time: 927 us; the launch traced here: 913 us
  local copies, waits for them, and re-layouts  217 us (23%)
  other arithmetic  215 us (23%)
  matrix products  185 us (20%)
  Pallas kernels  159 us (17%)
  waiting for transfers between devices  68.3 us (7%)
  starting transfers between devices  51.3 us (6%)
  between operations  17.5 us (2%)
    pallas_call x1, Pallas kernels, reduce_all(): pl.pallas_call(body, out_shape=[jax.ShapeDtypeStruct(shape, jnp.float32)...  159 us
    reduce_scatter x1, waiting for transfers between devices, on_device(): lax.psum_scatter(key_grad.reshape(full_shape).astype(jnp.bfloat16), ('row...  55 us
    reduce_sum x4, other arithmetic, scaled_norm(): return centre * lax.rsqrt(spread + norm_eps) * gain_vec  48.2 us
    reduce_sum x4, other arithmetic, scaled_norm(): centre = values - jnp.mean(values, axis=-1, keepdims=True)  43.6 us
    ppermute x8, starting transfers between devices, with_edges(): before = lax.ppermute(value[:, length - 1:], axes, up)  40.7 us
    reduce_sum x4, other arithmetic, scaled_norm(): spread = jnp.mean(centre * centre, axis=-1, keepdims=True)  39.2 us
    conv_general_dilated x4, matrix products, smooth_forward(): lax.conv_general_dilated(padded, kernel, (1, 1), ((0, 0), (1, 1)), dimens...  27.7 us
    conv_general_dilated x4, matrix products, smooth_backward(): lax.conv_general_dilated(padded, upstream, (1, 1), ((0, 0), (1, 1)), dime...  26.5 us
  transfers between devices with their start and end apart: 20, of which 3 were waited for; matrix products, arithmetic and copies ran while one was open for 47% of the time, Pallas kernels for 0%

profile of v1, /device:TPU:1, one launch (start us, length us, event | category | flops | bytes accessed | tf_op | source)
XLA Modules:
  0.0 913.2 jit_solution(16050759002065271423)
XLA Ops:
  30.2 4.3 copy.508
  37.9 4.3 copy.507
  54.1 4.6 fusion.272
  61.0 5.9 squeeze.38
  66.9 8.6 fusion.292
  75.5 13.3 %copy.418 = f32[12,2,64,16,64]{4,3,2,1,0:T(8,128)} copy(f32[12,2,64,16,64]{2,4,3,1,0:T(8,128)} %get-tuple-element.597) | data formatting | bytes 12582912 | tf_op jit(solution)/shard_map/while/body/eval_jaxpr/add | solution.py:352
  88.9 6.8 exponential_reduce_fusion
  95.7 10.9 %all-gather.3.cloned.1.call-done = bf16[1,16,64,768]{3,2,0,1:T(8,128)(2,1)} async-done(((bf16[1,2,64,768]{3,2,0,1:T(8,128)(2,1)}), bf16[1,16,64,768]{3,2,0,1:T(8,128)(2,1)}) %all-gather.3.cloned.1.call-update) | async-done | bytes 1572880 | tf_op jit(solution)/shard_map/all_gather | solution.py:620
  106.7 5.2 copy.410
  111.9 4.5 reshape.2081
  116.4 12.1 %reshape.2082 = f32[12,128,1024]{2,1,0:T(8,128)} reshape(f32[12,2,64,16,64]{4,3,2,1,0:T(8,128)} %copy.418) | data formatting | bytes 12582912 | tf_op jit(solution)/shard_map/while/body/eval_jaxpr/reshape | solution.py:353
  128.6 4.2 fusion.90
  134.2 4.3 fusion.165
  138.6 4.5 multiply_convert_fusion.2
  147.0 4.7 collective-permute-start.12
  200.3 5.5 reshape.2099
  211.2 5.2 collective-permute-start.8
  223.6 4.9 collective-permute-start.14
  239.9 4.1 collective-permute-start
  249.7 6.7 collective-permute-start.10
  257.3 4.5 fusion.297
  261.9 7.6 multiply_reduce_fusion.10
  269.5 9.5 %multiply_reduce_fusion.8 = (f32[256]{0:T(256)}, f32[4,128]{1,0:T(4,128)S(1)}) fusion(f32[4,128]{1,0:T(4,128)S(1)} %fusion.231, bf16[1,4,128,256]{3,2,1,0:T(8,128)(2,1)S(1)} %copy-done.53, f32[4,128]{1,0:T(4,128)S(1)} %copy-done.160, f32[1,4,128,256]{3,0,2,1:T(1,128)S(1)} %get-tuple-element.610, f32[4,128]{1,0:T(4,128)S(1)} %broadcast_multiply_fusion.3, ...), kind=kLoop, calls=%fused_computation.230 | loop fusion | flops 1178880 | bytes 796672 | tf_op jit(solution)/shard_map/transpose(jvp())/reduce_sum | solution.py:287
  279.0 8.2 fusion.269
  287.9 5.1 fusion.127
  295.3 6.9 collective-permute-start.6
  308.2 4.7 copy.431
  312.9 21.1 %fusion.295 = (f32[8,256]{1,0:T(8,128)S(1)}, f32[1,8,256,256]{3,0,2,1:T(1,128)S(1)}) fusion(bf16[1,10,256,256]{3,0,2,1:T(2,128)(2,1)} %copy.431, bf16[3,3,256,256]{3,2,1,0:T(8,128)(2,1)} %bitcast.585), kind=kOutput, calls=%fused_computation.531 | convolution fusion | flops 2410149888 | bytes 4595712 | tf_op jit(solution)/shard_map/conv_general_dilated | solution.py:379
  334.0 29.4 %multiply_reduce_fusion.3 = f32[8,256]{1,0:T(8,128)S(1)} fusion(f32[1,8,256,256]{3,0,2,1:T(1,128)S(1)} %get-tuple-element.606, f32[8,256]{1,0:T(8,128)S(1)} %broadcast_multiply_fusion), kind=kLoop, calls=%fused_computation.63 | loop fusion | flops 1570816 | bytes 2113536 | tf_op jit(solution)/shard_map/jvp()/reduce_sum | solution.py:286
  363.4 35.2 %multiply_reduce_fusion.1 = (f32[256]{0:T(256)}, f32[8,256]{1,0:T(8,128)S(1)}) fusion(f32[8,256]{1,0:T(8,128)S(1)} %fusion.229, bf16[1,8,256,256]{3,2,1,0:T(8,128)(2,1)S(1)} %copy-done.22, f32[8,256]{1,0:T(8,128)S(1)} %copy-done.128, f32[1,8,256,256]{3,0,2,1:T(1,128)S(1)} %get-tuple-element.606, f32[8,256]{1,0:T(8,128)S(1)} %broadcast_multiply_fusion, ...), kind=kLoop, calls=%fused_computation.59 | loop fusion | flops 4716288 | bytes 3180544 | tf_op jit(solution)/shard_map/transpose(jvp())/reduce_sum | solution.py:287
  398.6 32.8 %fusion.267 = (f32[8,256]{1,0:T(8,128)S(1)}, f32[1,8,256,256]{3,0,2,1:T(1,128)S(1)}) fusion(f32[8,256]{1,0:T(8,128)S(1)} %multiply_multiply_fusion.16, f32[1,8,256,256]{3,0,2,1:T(1,128)S(1)} %get-tuple-element.606, f32[8,256]{1,0:T(8,128)S(1)} %broadcast_multiply_fusion, f32[8,256]{1,0:T(8,128)S(1)} %fusion.229, f32[256]{0:T(256)S(1)} %bitcast.637, ...), kind=kLoop, calls=%fused_computation.504 | loop fusion | flops 4716544 | bytes 5284864 | tf_op jit(solution)/shard_map/transpose(jvp())/reduce_sum | solution.py:285
  434.3 16.9 %fusion.306 = f32[3,3,256,256]{3,2,1,0:T(8,128)} fusion(bf16[1,10,256,256]{3,0,2,1:T(2,128)(2,1)S(1)} %copy-done.50, bf16[1,8,256,256]{3,0,2,1:T(2,128)(2,1)S(1)} %add_convert_fusion.1), kind=kOutput, calls=%fused_computation.542 | convolution fusion | flops 2409627648 | bytes 4718592 | tf_op jit(solution)/shard_map/conv_general_dilated | solution.py:402
  452.6 4.9 fusion.303
  467.0 4.7 collective-permute-start.2
  481.8 17.1 %fusion.302 = (f32[256]{0:T(256)S(1)}, f32[1,8,256,256]{3,0,2,1:T(1,128)}) fusion(bf16[3,3,256,256]{3,2,1,0:T(8,128)(2,1)S(1)} %bitcast.586, bf16[1,1,256,256]{3,0,2,1:T(2,128)(2,1)} %collective-permute-done.3, bf16[1,8,256,256]{3,0,2,1:T(2,128)(2,1)} %copy-done.38, bf16[1,1,256,256]{3,0,2,1:T(2,128)(2,1)} %collective-permute-done.2), kind=kOutput, calls=%fused_computation.538 | convolution fusion | flops 2414083840 | bytes 4588544 | tf_op jit(solution)/shard_map/conv_general_dilated | solution.py:394
  498.9 6.2 copy.432
  515.5 4.4 fusion.258
  525.7 5.7 convert_reduce_fusion.1
  541.3 5.5 fusion.48
  551.8 5.3 convert_element_type.603
  557.1 5.0 copy.463
  562.1 6.8 multiply_convert_fusion
  568.9 9.5 %reshape.2163 = f32[12,2,64,16,64]{4,3,2,1,0:T(8,128)} reshape(bf16[12,128,1024]{2,1,0:T(8,128)(2,1)} %multiply_convert_fusion) | data formatting | bytes 9437184 | tf_op jit(solution)/shard_map/while/body/eval_jaxpr/convert_element_type | solution.py:360
  584.3 5.1 copy.462
  594.5 9.4 %fusion.257 = (f32[12,2,64,64]{3,2,1,0:T(8,128)}, f32[12,2,64,16]{3,2,1,0:T(8,128)}) fusion(f32[12,2,64,16,64]{4,3,2,1,0:T(8,128)} %reshape.2163), kind=kLoop, calls=%fused_computation.496 | loop fusion | flops 3022848 | bytes 6782976 | tf_op jit(solution)/shard_map/while/body/eval_jaxpr/reduce_sum | solution.py:361
  621.7 4.2 fusion.92
  649.3 55.0 %reduce-scatter.3.cloned.1.call-done = bf16[1,2,64,768]{3,2,1,0:T(8,128)(2,1)} async-done(((bf16[1,16,64,768]{3,2,1,0:T(8,128)(2,1)}), bf16[1,2,64,768]{3,2,1,0:T(8,128)(2,1)}) %reduce-scatter.3.cloned.1.call-update) | async-done | bytes 196624 | tf_op jit(solution)/shard_map/reduce_scatter | solution.py:711
  720.4 159.0 %reduce_grads.1 = (f32[288,256]{1,0:T(8,128)}, f32[96,768]{1,0:T(8,128)}, f32[48,1536]{1,0:T(8,128)}, f32[96,768]{1,0:T(8,128)}, f32[48,1152]{1,0:T(8,128)}, /*i...) custom-call(bf16[2,2,2,2,2,288,256]{6,5,4,3,2,1,0:T(8,128)(2,1)} %bitcast.555, ...), custom_call_target="tpu_custom_call" | custom-call | tf_op jit(solution)/shard_map/reduce_grads/pallas_call | solution.py:189
  (840 shorter events, 281.4 us)
Async XLA Ops:
  7.2 126.2 %copy-start = (bf16[768,768]{1,0:T(8,128)(2,1)S(1)}, bf16[768,768]{1,0:T(8,128)(2,1)}, u32[]{:S(2)}) copy-start(bf16[768,768]{1,0:T(8,128)(2,1)} %param.79) | copy-start | bytes 3538948
  7.2 53.8 %all-gather.5.cloned.1.call-start = ((), (), s32[]{:S(2)}) async-start(), calls=%async_computation.3 | async-start | bytes 1769472 | tf_op jit(solution)/shard_map/all_gather | solution.py:619
  15.1 91.5 %all-gather.3.cloned.1.call-start = ((), (), s32[]{:S(2)}) async-start(), calls=%async_computation.2 | async-start | bytes 1769472 | tf_op jit(solution)/shard_map/all_gather | solution.py:620
  15.9 633.3 %reduce-scatter.5.cloned.1.call-start = ((), (), s32[]{:S(2)}) async-start(), calls=%async_computation.5 | async-start | bytes 1769472 | tf_op jit(solution)/shard_map/reduce_scatter | solution.py:717
  16.4 50.5 %copy-start.11 = (bf16[2,64,12,64]{3,2,1,0:T(8,128)(2,1)}, bf16[2,64,12,64]{3,2,1,0:T(8,128)(2,1)S(1)}, u32[]{:S(2)}) copy-start(bf16[2,64,12,64]{3,2,1,0:T(8,128)(2,1)S(1)} %squeeze.37) | copy-start | bytes 589828
  23.1 26.7 %copy-start.233 = (s32[2,16]{1,0:T(2,128)}, s32[2,16]{1,0:T(2,128)S(1)}, u32[]{:S(2)}) copy-start(s32[2,16]{1,0:T(2,128)S(1)} %subtract_add_fusion.1) | copy-start | bytes 388
  25.6 108.5 %copy-start.124 = (f32[768]{0:T(1024)}, f32[768]{0:T(1024)S(1)}, u32[]{:S(2)}) copy-start(f32[768]{0:T(1024)S(1)} %convert_element_type.519) | copy-start | bytes 9220
  26.3 107.8 %copy-start.110 = (f32[768]{0:T(1024)}, f32[768]{0:T(1024)S(1)}, u32[]{:S(2)}) copy-start(f32[768]{0:T(1024)S(1)} %convert_element_type.518) | copy-start | bytes 9220
  37.8 126.1 %copy-start.146 = (f32[384]{0:T(512)}, f32[384]{0:T(512)S(1)}, u32[]{:S(2)}) copy-start(f32[384]{0:T(512)S(1)} %convert_element_type.526) | copy-start | bytes 4612
  37.8 126.0 %copy-start.126 = (f32[384]{0:T(512)}, f32[384]{0:T(512)S(1)}, u32[]{:S(2)}) copy-start(f32[384]{0:T(512)S(1)} %convert_element_type.525) | copy-start | bytes 4612
  88.9 39.7 %copy-start.150 = (f32[12,128]{1,0:T(8,128)}, f32[12,128]{1,0:T(8,128)S(1)}, u32[]{:S(2)}) copy-start(f32[12,128]{1,0:T(8,128)S(1)} %sub.222) | copy-start | bytes 18436
  144.0 38.9 %copy-start.17 = (bf16[1,2,64,768]{3,2,1,0:T(8,128)(2,1)}, bf16[1,2,64,768]{3,2,1,0:T(8,128)(2,1)S(1)}, u32[]{:S(2)}) copy-start(bf16[1,2,64,768]{3,2,1,0:T(8,128)(2,1)S(1)} %get-tuple-element.616) | copy-start | bytes 589828
  145.7 64.1 %collective-permute-start.13 = (bf16[1,1,32,256]{3,2,1,0:T(8,128)(2,1)}, bf16[1,1,32,256]{3,2,1,0:T(8,128)(2,1)}, u32[]{:S(2)}, u32[]{:S(2)}) collective-permute-start(bf16[1,1,32,256]{3,2,1,0:T(8,128)(2,1)} %fusion.222), channel_id=1, source_target_pairs={{1,0},{2,1},{3,2},{4,3},{5,4},{6,5},{7,6},{9,8},{10,9},{11,10},{12... | collective-permute-start | bytes 49160 | tf_op jit(solution)/shard_map/ppermute | solution.py:270
  147.0 64.1 %collective-permute-start.12 = (bf16[1,1,32,256]{3,2,1,0:T(8,128)(2,1)}, bf16[1,1,32,256]{3,2,1,0:T(8,128)(2,1)}, u32[]{:S(2)}, u32[]{:S(2)}) collective-permute-start(bf16[1,1,32,256]{3,2,1,0:T(8,128)(2,1)} %fusion.222), channel_id=1, source_target_pairs={{0,1},{1,2},{2,3},{3,4},{4,5},{5,6},{6,7},{8,9},{9,10},{10,11},{11... | collective-permute-start | bytes 49160 | tf_op jit(solution)/shard_map/ppermute | solution.py:269
  158.4 98.0 %collective-permute-start.4 = (bf16[1,1,128,256]{3,2,1,0:T(8,128)(2,1)}, bf16[1,1,128,256]{3,2,1,0:T(8,128)(2,1)}, u32[]{:S(2)}, u32[]{:S(2)}) collective-permute-start(bf16[1,1,128,256]{3,2,1,0:T(8,128)(2,1)} %get-tuple-element.552), channel_id=1, source_target_pairs={{0,1},{1,2},{2,3},{3,4},{4,5},{5,6},{6,7},{8,9},{9,10},{10,11},{11... | collective-permute-start | bytes 196616 | tf_op jit(solution)/shard_map/ppermute | solution.py:269
  181.6 125.4 %collective-permute-start.1 = (bf16[1,1,256,256]{2,3,1,0:T(8,128)(2,1)}, bf16[1,1,256,256]{2,3,1,0:T(8,128)(2,1)}, u32[]{:S(2)}, u32[]{:S(2)}) collective-permute-start(bf16[1,1,256,256]{2,3,1,0:T(8,128)(2,1)} %get-tuple-element.539), channel_id=1, source_target_pairs={{1,0},{2,1},{3,2},{4,3},{5,4},{6,5},{7,6},{9,8},{10,9},{11,10},{12... | collective-permute-start | bytes 393224 | tf_op jit(solution)/shard_map/ppermute | solution.py:270
  190.2 59.5 %collective-permute-start.5 = (bf16[1,1,128,256]{3,2,1,0:T(8,128)(2,1)}, bf16[1,1,128,256]{3,2,1,0:T(8,128)(2,1)}, u32[]{:S(2)}, u32[]{:S(2)}) collective-permute-start(bf16[1,1,128,256]{3,2,1,0:T(8,128)(2,1)} %get-tuple-element.553), channel_id=1, source_target_pairs={{1,0},{2,1},{3,2},{4,3},{5,4},{6,5},{7,6},{9,8},{10,9},{11,10},{12... | collective-permute-start | bytes 196616 | tf_op jit(solution)/shard_map/ppermute | solution.py:270
  209.9 12.3 %collective-permute-start.9 = (bf16[1,1,64,256]{3,2,1,0:T(8,128)(2,1)S(1)}, bf16[1,1,64,256]{3,2,1,0:T(8,128)(2,1)S(1)}, u32[]{:S(2)}, u32[]{:S(2)}) collective-permute-start(bf16[1,1,64,256]{3,2,1,0:T(8,128)(2,1)S(1)} %copy-done.155), channel_id=1, source_target_pairs={{1,0},{2,1},{3,2},{4,3},{5,4},{6,5},{7,6},{9,8},{10,9},{11,10},{12... | collective-permute-start | bytes 98312 | tf_op jit(solution)/shard_map/ppermute | solution.py:270
  211.2 12.5 %collective-permute-start.8 = (bf16[1,1,64,256]{3,2,1,0:T(8,128)(2,1)S(1)}, bf16[1,1,64,256]{3,2,1,0:T(8,128)(2,1)S(1)}, u32[]{:S(2)}, u32[]{:S(2)}) collective-permute-start(bf16[1,1,64,256]{3,2,1,0:T(8,128)(2,1)S(1)} %copy-done.154), channel_id=1, source_target_pairs={{0,1},{1,2},{2,3},{3,4},{4,5},{5,6},{6,7},{8,9},{9,10},{10,11},{11... | collective-permute-start | bytes 98312 | tf_op jit(solution)/shard_map/ppermute | solution.py:269
  222.2 17.7 %collective-permute-start.15 = (bf16[1,1,32,256]{3,0,2,1:T(2,128)(2,1)S(1)}, bf16[1,1,32,256]{3,0,2,1:T(2,128)(2,1)S(1)}, u32[]{:S(2)}, u32[]{:S(2)}) collective-permute-start(bf16[1,1,32,256]{3,0,2,1:T(2,128)(2,1)S(1)} %add_convert_fusion.19), channel_id=1, source_target_pairs={{1,0},{2,1},{3,2},{4,3},{5,4},{6,5},{7,6},{9,8},{10,9},{11,10},{12... | collective-permute-start | bytes 49160 | tf_op jit(solution)/shard_map/ppermute | solution.py:270
  223.6 20.4 %collective-permute-start.14 = (bf16[1,1,32,256]{3,0,2,1:T(2,128)(2,1)S(1)}, bf16[1,1,32,256]{3,0,2,1:T(2,128)(2,1)S(1)}, u32[]{:S(2)}, u32[]{:S(2)}) collective-permute-start(bf16[1,1,32,256]{3,0,2,1:T(2,128)(2,1)S(1)} %add_convert_fusion.19), channel_id=1, source_target_pairs={{0,1},{1,2},{2,3},{3,4},{4,5},{5,6},{6,7},{8,9},{9,10},{10,11},{11... | collective-permute-start | bytes 49160 | tf_op jit(solution)/shard_map/ppermute | solution.py:269
  239.9 16.4 %copy-start.62 = (bf16[1,4,128,256]{3,2,1,0:T(8,128)(2,1)S(1)}, bf16[1,4,128,256]{3,2,1,0:T(8,128)(2,1)}, u32[]{:S(2)}) copy-start(bf16[1,4,128,256]{3,2,1,0:T(8,128)(2,1)} %copy-done.61) | copy-start | bytes 786436
  239.9 67.1 %collective-permute-start = (bf16[1,1,256,256]{2,3,1,0:T(8,128)(2,1)}, bf16[1,1,256,256]{2,3,1,0:T(8,128)(2,1)}, u32[]{:S(2)}, u32[]{:S(2)}) collective-permute-start(bf16[1,1,256,256]{2,3,1,0:T(8,128)(2,1)} %get-tuple-element.538), channel_id=1, source_target_pairs={{0,1},{1,2},{2,3},{3,4},{4,5},{5,6},{6,7},{8,9},{9,10},{10,11},{11... | collective-permute-start | bytes 393224 | tf_op jit(solution)/shard_map/ppermute | solution.py:269
  246.1 49.2 %collective-permute-start.11 = (bf16[1,1,64,256]{3,0,2,1:T(2,128)(2,1)}, bf16[1,1,64,256]{3,0,2,1:T(2,128)(2,1)}, u32[]{:S(2)}, u32[]{:S(2)}) collective-permute-start(bf16[1,1,64,256]{3,0,2,1:T(2,128)(2,1)} %get-tuple-element.565), channel_id=1, source_target_pairs={{1,0},{2,1},{3,2},{4,3},{5,4},{6,5},{7,6},{9,8},{10,9},{11,10},{12... | collective-permute-start | bytes 98312 | tf_op jit(solution)/shard_map/ppermute | solution.py:270
  249.7 52.5 %collective-permute-start.10 = (bf16[1,1,64,256]{3,0,2,1:T(2,128)(2,1)}, bf16[1,1,64,256]{3,0,2,1:T(2,128)(2,1)}, u32[]{:S(2)}, u32[]{:S(2)}) collective-permute-start(bf16[1,1,64,256]{3,0,2,1:T(2,128)(2,1)} %get-tuple-element.564), channel_id=1, source_target_pairs={{0,1},{1,2},{2,3},{3,4},{4,5},{5,6},{6,7},{8,9},{9,10},{10,11},{11... | collective-permute-start | bytes 98312 | tf_op jit(solution)/shard_map/ppermute | solution.py:269
  287.9 14.3 %copy-start.77 = (bf16[1,2304,256]{2,1,0:T(8,128)(2,1)S(1)}, bf16[1,2304,256]{2,1,0:T(8,128)(2,1)}, u32[]{:S(2)}) copy-start(bf16[1,2304,256]{2,1,0:T(8,128)(2,1)} %get-tuple-element.522) | copy-start | bytes 3538948
  294.0 158.6 %collective-permute-start.7 = (bf16[1,1,128,256]{3,0,2,1:T(2,128)(2,1)}, bf16[1,1,128,256]{3,0,2,1:T(2,128)(2,1)}, u32[]{:S(2)}, u32[]{:S(2)}) collective-permute-start(bf16[1,1,128,256]{3,0,2,1:T(2,128)(2,1)} %get-tuple-element.541), channel_id=1, source_target_pairs={{1,0},{2,1},{3,2},{4,3},{5,4},{6,5},{7,6},{9,8},{10,9},{11,10},{12... | collective-permute-start | bytes 196616 | tf_op jit(solution)/shard_map/ppermute | solution.py:270
  295.3 157.3 %collective-permute-start.6 = (bf16[1,1,128,256]{3,0,2,1:T(2,128)(2,1)}, bf16[1,1,128,256]{3,0,2,1:T(2,128)(2,1)}, u32[]{:S(2)}, u32[]{:S(2)}) collective-permute-start(bf16[1,1,128,256]{3,0,2,1:T(2,128)(2,1)} %get-tuple-element.540), channel_id=1, source_target_pairs={{0,1},{1,2},{2,3},{3,4},{4,5},{5,6},{6,7},{8,9},{9,10},{10,11},{11... | collective-permute-start | bytes 196616 | tf_op jit(solution)/shard_map/ppermute | solution.py:269
  333.9 29.4 %copy-start.22 = (bf16[1,8,256,256]{3,2,1,0:T(8,128)(2,1)S(1)}, bf16[1,8,256,256]{3,2,1,0:T(8,128)(2,1)}, u32[]{:S(2)}) copy-start(bf16[1,8,256,256]{3,2,1,0:T(8,128)(2,1)} %constant_dynamic-slice_fusion.6) | copy-start | bytes 3145732
  334.0 29.4 %copy-start.128 = (f32[8,256]{1,0:T(8,128)S(1)}, f32[8,256]{1,0:T(8,128)}, u32[]{:S(2)}) copy-start(f32[8,256]{1,0:T(8,128)} %copy.426) | copy-start | bytes 24580
  334.0 29.4 %copy-start.198 = (f32[1,256]{1,0:T(1,128)S(1)}, f32[1,256]{1,0:T(1,128)}, u32[]{:S(2)}) copy-start(f32[1,256]{1,0:T(1,128)} %get-tuple-element.586) | copy-start | bytes 3076
  434.3 17.0 %copy-start.38 = (bf16[1,8,256,256]{3,0,2,1:T(2,128)(2,1)}, bf16[1,8,256,256]{3,0,2,1:T(2,128)(2,1)S(1)}, u32[]{:S(2)}) copy-start(bf16[1,8,256,256]{3,0,2,1:T(2,128)(2,1)S(1)} %add_convert_fusion.1) | copy-start | bytes 3145732
  434.3 18.3 %copy-start.75 = (bf16[1,2304,256]{2,1,0:T(8,128)(2,1)S(1)}, bf16[1,2304,256]{2,1,0:T(8,128)(2,1)}, u32[]{:S(2)}) copy-start(bf16[1,2304,256]{2,1,0:T(8,128)(2,1)} %get-tuple-element.523) | copy-start | bytes 3538948
  434.3 18.3 %copy-start.82 = (bf16[1,4,128,256]{3,0,2,1:T(2,128)(2,1)S(1)}, bf16[1,4,128,256]{3,0,2,1:T(2,128)(2,1)}, u32[]{:S(2)}) copy-start(bf16[1,4,128,256]{3,0,2,1:T(2,128)(2,1)} %copy-done.81) | copy-start | bytes 786436
  465.7 16.0 %collective-permute-start.3 = (bf16[1,1,256,256]{3,0,2,1:T(2,128)(2,1)}, bf16[1,1,256,256]{3,0,2,1:T(2,128)(2,1)}, u32[]{:S(2)}, u32[]{:S(2)}) collective-permute-start(bf16[1,1,256,256]{3,0,2,1:T(2,128)(2,1)} %get-tuple-element.533), channel_id=1, source_target_pairs={{1,0},{2,1},{3,2},{4,3},{5,4},{6,5},{7,6},{9,8},{10,9},{11,10},{12... | collective-permute-start | bytes 393224 | tf_op jit(solution)/shard_map/ppermute | solution.py:270
  467.0 14.8 %collective-permute-start.2 = (bf16[1,1,256,256]{3,0,2,1:T(2,128)(2,1)}, bf16[1,1,256,256]{3,0,2,1:T(2,128)(2,1)}, u32[]{:S(2)}, u32[]{:S(2)}) collective-permute-start(bf16[1,1,256,256]{3,0,2,1:T(2,128)(2,1)} %get-tuple-element.532), channel_id=1, source_target_pairs={{0,1},{1,2},{2,3},{3,4},{4,5},{5,6},{6,7},{8,9},{9,10},{10,11},{11... | collective-permute-start | bytes 393224 | tf_op jit(solution)/shard_map/ppermute | solution.py:269
  562.1 142.2 %reduce-scatter.3.cloned.1.call-start = ((), (), s32[]{:S(2)}) async-start(), calls=%async_computation.4 | async-start | bytes 1769472 | tf_op jit(solution)/shard_map/reduce_scatter | solution.py:711
  646.5 57.8 %copy-start.24 = (bf16[1,2,64,768]{3,2,1,0:T(8,128)(2,1)S(1)}, bf16[1,2,64,768]{3,2,1,0:T(8,128)(2,1)}, u32[]{:S(2)}) copy-start(bf16[1,2,64,768]{3,2,1,0:T(8,128)(2,1)} %param.72) | copy-start | bytes 589828
  646.5 57.8 %copy-start.116 = (f32[768]{0:T(1024)S(1)}, f32[768]{0:T(1024)}, u32[]{:S(2)}) copy-start(f32[768]{0:T(1024)} %copy-done.115) | copy-start | bytes 9220
  646.5 57.8 %copy-start.118 = (bf16[1,2,64,768]{3,2,1,0:T(8,128)(2,1)S(1)}, bf16[1,2,64,768]{3,2,1,0:T(8,128)(2,1)}, u32[]{:S(2)}) copy-start(bf16[1,2,64,768]{3,2,1,0:T(8,128)(2,1)} %convert_element_type.596) | copy-start | bytes 589828
  646.5 57.8 %copy-start.141 = (f32[2,64]{1,0:T(2,128)S(1)}, f32[2,64]{1,0:T(2,128)}, u32[]{:S(2)}) copy-start(f32[2,64]{1,0:T(2,128)} %copy-done.140) | copy-start | bytes 1540
  649.3 58.7 %copy-start.189 = (f32[2,64]{1,0:T(2,128)S(1)}, f32[2,64]{1,0:T(2,128)}, u32[]{:S(2)}) copy-start(f32[2,64]{1,0:T(2,128)} %copy-done.188) | copy-start | bytes 1540
  649.3 59.3 %copy-start.123 = (f32[768]{0:T(1024)S(1)}, f32[768]{0:T(1024)}, u32[]{:S(2)}) copy-start(f32[768]{0:T(1024)} %copy-done.122) | copy-start | bytes 9220
  649.3 59.3 %copy-start.143 = (f32[2,64]{1,0:T(2,128)S(1)}, f32[2,64]{1,0:T(2,128)}, u32[]{:S(2)}) copy-start(f32[2,64]{1,0:T(2,128)} %copy-done.142) | copy-start | bytes 1540
  649.3 59.2 %copy-start.117 = (bf16[1,2,64,768]{3,2,1,0:T(8,128)(2,1)S(1)}, bf16[1,2,64,768]{3,2,1,0:T(8,128)(2,1)}, u32[]{:S(2)}) copy-start(bf16[1,2,64,768]{3,2,1,0:T(8,128)(2,1)} %reduce-scatter.5.cloned.1.call-done) | copy-start | bytes 589828
  720.4 173.0 %copy-start.49 = (bf16[2,64,768]{2,1,0:T(8,128)(2,1)S(1)}, bf16[2,64,768]{2,1,0:T(8,128)(2,1)}, u32[]{:S(2)}) copy-start(bf16[2,64,768]{2,1,0:T(8,128)(2,1)} %copy-done.47) | copy-start | bytes 589828
  879.3 16.0 %copy-start.112 = (f32[48,1152]{1,0:T(8,128)S(1)}, f32[48,1152]{1,0:T(8,128)}, u32[]{:S(2)}) copy-start(f32[48,1152]{1,0:T(8,128)} %get-tuple-element.296) | copy-start | bytes 663556
  882.1 15.3 %copy-start.109 = (f32[48,1536]{1,0:T(8,128)S(1)}, f32[48,1536]{1,0:T(8,128)}, u32[]{:S(2)}) copy-start(f32[48,1536]{1,0:T(8,128)} %get-tuple-element.298) | copy-start | bytes 884740
  (213 other events, 1106.6 us)
Sparse Core Ops, SparseCore 0:
  15.2 45.7 all-gather.4
  63.7 42.9 all-gather.2
  562.2 73.6 reduce-scatter.4
  639.6 64.6 reduce-scatter.2
